TPU v7x, 512 devices: a whole 4x8x8 slice. The times are simulated.
512 devices in a mesh: img: 16 (over z, core), seq: 8 (over y), head: 4 (over x).
Axes of the slice: x: 4, y: 8, z: 8, core: 2. Of those that a mesh axis runs over, the one named last changes fastest.
Arguments:
- queries: bfloat16 [16, 1024, 4096], P('img', 'seq', 'head'), may hold values from -6 to 6
- out_grad: bfloat16 [16, 1024, 4096], P('img', 'seq', 'head'), may hold values from -16 to 16
- text_len: int32 [16], P('img'), may hold values from 256 to 1024, as said below
- image_keys: bfloat16 [32, 1600, 512], P('img', ('seq', 'head')), may hold values from -6 to 6
- image_values: bfloat16 [32, 1600, 512], P('img', ('seq', 'head')), may hold values from -6 to 6
- tile_counts: int32 [16], P('img'), may hold values from 1 to 4, as said below
- tile_slots: int32 [16, 4], P('img'), may hold values from -1 to 31, as said below
- gate_param: float32 [1], replicated, may hold values from 0.3 to 1.5
Outputs:
- query_grad: bfloat16 [16, 1024, 4096], P('img', 'seq', 'head')
- key_grad: bfloat16 [32, 1600, 512], P('img', ('seq', 'head'))
- value_grad: bfloat16 [32, 1600, 512], P('img', ('seq', 'head'))
Inputs may be any that keep to these rules, and one draw needn't show every extreme that they name: `tile_counts`: each sample has 1 to 4 tiles, some sample exactly 4; the counts sum to 32. `tile_slots`: entry j of a sample is the slot of its tile j for j below its count and -1 beyond; every slot appears exactly once. `text_len`: some sample has all 1024 positions valid.
All inputs are finite; a program needn't handle non-finite values.
Results may differ from a plain program's by a relative error of at most 0.019.
Values may be sent and summed in bfloat16 or wider, within the bound.
A program may use at most 64 MiB of HBM per device.

v0:
```python
import jax
import jax.numpy as jnp
from jax import lax
from jax.sharding import PartitionSpec as P

HEAD_DIM = 128
MAX_TILES = 4
SLOT_DEV = 2
TEXT_DEV = 128
GROUP = 8


def place_tiles(tiles, slot_index, usable, slot_total):
    holder = jnp.zeros((slot_total,) + tiles.shape[1:], jnp.bfloat16)
    kept = jnp.where(usable[:, None, None], tiles, jnp.zeros_like(tiles))
    return holder.at[slot_index].add(kept)


def on_device(
    queries, out_grad, text_len, image_keys, image_values, tile_counts, tile_slots, gate_param
):
    img_size = lax.axis_size("img")
    tile_count = tile_counts[0]
    usable = jnp.arange(MAX_TILES) < tile_count
    slot_index = jnp.maximum(tile_slots[0], 0)
    empty_tiles = jnp.zeros((MAX_TILES,) + image_keys.shape[1:], jnp.bfloat16)
    piece_keys = lax.all_gather(image_keys, "img", axis=0, tiled=True)
    piece_values = lax.all_gather(image_values, "img", axis=0, tiled=True)
    span = piece_keys.shape[0]
    inside_mask = (usable & (slot_index >= 0) & (slot_index < span))[:, None, None]
    clipped = jnp.clip(slot_index, 0, span - 1)
    new_keys = jnp.where(inside_mask, piece_keys[clipped], empty_tiles)
    new_values = jnp.where(inside_mask, piece_values[clipped], empty_tiles)
    own_keys = new_keys
    own_values = new_values
    own_keys, own_values = (
        lax.all_to_all(own_keys, "head", split_axis=2, concat_axis=1, tiled=True),
        lax.all_to_all(own_values, "head", split_axis=2, concat_axis=1, tiled=True),
    )
    full_keys, full_values = (
        lax.all_gather(own_keys, "seq", axis=1, tiled=True),
        lax.all_gather(own_values, "seq", axis=1, tiled=True),
    )
    gate_multiplier = jnp.tanh(gate_param[0])
    score_scale = HEAD_DIM ** (-0.5)
    row_start = lax.axis_index("seq") * TEXT_DEV
    row_live = row_start + jnp.arange(TEXT_DEV) < text_len[0]
    query_rows = queries[0].reshape(TEXT_DEV, GROUP, HEAD_DIM)
    grad_live = jnp.where(row_live[:, None], out_grad[0], jnp.zeros_like(out_grad[0]))
    grad_rows = grad_live.reshape(TEXT_DEV, GROUP, HEAD_DIM)

    def tile_terms(position):
        key_tile = lax.dynamic_index_in_dim(full_keys, position, 0, keepdims=False)
        value_tile = lax.dynamic_index_in_dim(full_values, position, 0, keepdims=False)
        scores = (
            jnp.einsum("rgd,kd->grk", query_rows, key_tile, preferred_element_type=jnp.float32)
            * score_scale
        )
        grad_probs = jnp.einsum(
            "rgd,kd->grk", grad_rows, value_tile, preferred_element_type=jnp.float32
        )
        return (key_tile, scores, grad_probs)

    def first_sweep(position, sweep_state):
        row_max, row_total, row_cross = sweep_state
        key_tile, scores, grad_probs = tile_terms(position)
        new_max = jnp.maximum(row_max, jnp.max(scores, axis=-1))
        shrink = jnp.exp(row_max - new_max)
        exponent = jnp.exp(scores - new_max[..., None])
        new_total = row_total * shrink + jnp.sum(exponent, axis=-1)
        new_cross = row_cross * shrink + jnp.sum(exponent * grad_probs, axis=-1)
        return (new_max, new_total, new_cross)

    row_zeros = jnp.zeros((GROUP, TEXT_DEV), jnp.float32)
    start_state = (jnp.full((GROUP, TEXT_DEV), -1e30, jnp.float32), row_zeros, row_zeros)
    row_max, row_total, row_cross = lax.fori_loop(0, tile_count, first_sweep, start_state)
    delta_rows = row_cross / row_total

    def second_sweep(position, sweep_state):
        query_acc, key_part, value_part = sweep_state
        key_tile, scores, grad_probs = tile_terms(position)
        probs = jnp.exp(scores - row_max[..., None]) / row_total[..., None]
        weights = probs.astype(jnp.bfloat16)
        score_grads = (
            gate_multiplier * probs * (grad_probs - delta_rows[..., None]) * score_scale
        ).astype(jnp.bfloat16)
        query_acc = query_acc + jnp.einsum(
            "grk,kd->rgd", score_grads, key_tile, preferred_element_type=jnp.float32
        )
        value_term = (
            gate_multiplier
            * jnp.einsum("grk,rgd->kd", weights, grad_rows, preferred_element_type=jnp.float32)
        ).astype(jnp.bfloat16)
        key_term = jnp.einsum(
            "grk,rgd->kd", score_grads, query_rows, preferred_element_type=jnp.float32
        ).astype(jnp.bfloat16)
        key_part = lax.dynamic_update_index_in_dim(key_part, key_term, position, 0)
        value_part = lax.dynamic_update_index_in_dim(value_part, value_term, position, 0)
        return (query_acc, key_part, value_part)

    zero_parts = jnp.zeros((MAX_TILES, full_keys.shape[1], HEAD_DIM), jnp.bfloat16)
    zero_query = jnp.zeros((TEXT_DEV, GROUP, HEAD_DIM), jnp.float32)
    query_acc, key_part, value_part = lax.fori_loop(
        0, tile_count, second_sweep, (zero_query, zero_parts, zero_parts)
    )
    key_sum, value_sum = (
        lax.psum_scatter(key_part, "seq", scatter_dimension=1, tiled=True).astype(jnp.float32),
        lax.psum_scatter(value_part, "seq", scatter_dimension=1, tiled=True).astype(jnp.float32),
    )
    key_grads = key_sum.astype(jnp.bfloat16)
    value_grads = value_sum.astype(jnp.bfloat16)
    slot_total = SLOT_DEV * img_size
    held_keys = place_tiles(key_grads, slot_index, usable, slot_total)
    held_values = place_tiles(value_grads, slot_index, usable, slot_total)
    back_keys, back_values = (
        lax.all_to_all(
            lax.all_to_all(held_keys, "img", split_axis=0, concat_axis=0, tiled=True),
            "head",
            split_axis=1,
            concat_axis=2,
            tiled=True,
        ),
        lax.all_to_all(
            lax.all_to_all(held_values, "img", split_axis=0, concat_axis=0, tiled=True),
            "head",
            split_axis=1,
            concat_axis=2,
            tiled=True,
        ),
    )
    owner_shape = (img_size, SLOT_DEV) + back_keys.shape[1:]
    key_out = back_keys.reshape(owner_shape).astype(jnp.float32).sum(axis=0).astype(jnp.bfloat16)
    value_out = (
        back_values.reshape(owner_shape).astype(jnp.float32).sum(axis=0).astype(jnp.bfloat16)
    )
    query_out = query_acc.reshape(1, TEXT_DEV, GROUP * HEAD_DIM).astype(jnp.bfloat16)
    return (query_out, key_out, value_out)


def solution(mesh):
    return jax.shard_map(
        on_device,
        mesh=mesh,
        in_specs=(
            P("img", "seq", "head"),
            P("img", "seq", "head"),
            P("img"),
            P("img", ("seq", "head"), None),
            P("img", ("seq", "head"), None),
            P("img"),
            P("img", None),
            P(),
        ),
        out_specs=(
            P("img", "seq", "head"),
            P("img", ("seq", "head"), None),
            P("img", ("seq", "head"), None),
        ),
        check_vma=False,
    )
```

profile of v0, /device:TPU:1, one launch (start us, length us, event | category | flops | bytes accessed | tf_op | source)
XLA Modules:
  0.0 521.1 jit_solution(9661608436269819218)
XLA Ops:
  12.4 46.5 %all-gather.5.cloned.1.call-done = bf16[32,50,512]{2,1,0:T(8,128)(2,1)} async-done(((bf16[2,50,512]{2,1,0:T(8,128)(2,1)}), bf16[32,50,512]{2,1,0:T(8,128)(2,1)}) %all-gather.5.cloned.1.call-update) | async-done | bytes 1638416 | tf_op jit(solution)/shard_map/all_gather | solution.py:27
  61.0 41.5 %all-gather.9.cloned.1.call-done = bf16[32,50,512]{2,1,0:T(8,128)(2,1)} async-done(((bf16[2,50,512]{2,1,0:T(8,128)(2,1)}), bf16[32,50,512]{2,1,0:T(8,128)(2,1)}) %all-gather.9.cloned.1.call-update) | async-done | bytes 1638416 | tf_op jit(solution)/shard_map/all_gather | solution.py:28
  106.1 9.1 %all_to_all.76 = bf16[4,2,12800]{2,1,0:T(2,128)(2,1)S(1)} all-to-all(bf16[4,2,12800]{2,1,0:T(2,128)(2,1)S(1)} %reshape.144), channel_id=1, replica_groups=mesh['img'=16,'seq'=8,'head'=4] {'head'}, dimensions={0} | all-to-all | bytes 409600 | tf_op jit(solution)/shard_map/all_to_all | solution.py:38
  119.4 7.7 %all_to_all.77 = bf16[4,2,12800]{2,1,0:T(2,128)(2,1)S(1)} all-to-all(bf16[4,2,12800]{2,1,0:T(2,128)(2,1)S(1)} %reshape.142), channel_id=1, replica_groups=mesh['img'=16,'seq'=8,'head'=4] {'head'}, dimensions={0} | all-to-all | bytes 409600 | tf_op jit(solution)/shard_map/all_to_all | solution.py:37
  132.0 22.0 %all-gather.11.cloned.1.call-done = bf16[4,1600,128]{2,0,1:T(4,128)(2,1)} async-done(((bf16[4,200,128]{2,0,1:T(4,128)(2,1)}), bf16[4,1600,128]{2,0,1:T(4,128)(2,1)}) %all-gather.11.cloned.1.call-update) | async-done | bytes 1638416 | tf_op jit(solution)/shard_map/all_gather | solution.py:42
  156.8 41.3 %all-gather.7.cloned.1.call-done = bf16[4,1600,128]{2,0,1:T(4,128)(2,1)} async-done(((bf16[4,200,128]{2,0,1:T(4,128)(2,1)}), bf16[4,1600,128]{2,0,1:T(4,128)(2,1)}) %all-gather.7.cloned.1.call-update) | async-done | bytes 1638416 | tf_op jit(solution)/shard_map/all_gather | solution.py:41
  199.8 6.0 %while.28 = (s32[]{:T(128)}, f32[8,128]{1,0:T(8,128)S(1)}, f32[8,128]{1,0:T(8,128)S(1)}, f32[8,128]{1,0:T(8,128)S(1)}, s32[]{:T(128)}, /*index=5*/bf16[4,1600,12...) while((s32[]{:T(128)}, f32[8,128]{1,0:T(8,128)S(1)}, ...), condition=%wide.region_4.5_spmd, body=%wide.region_0.4_spmd.sunk | while | flops 853609472 | bytes 21078176 | solution.py:76
  208.6 9.4 %while.29 = (s32[]{:T(128)}, f32[128,8,128]{0,2,1:T(8,128)S(1)}, bf16[4,1600,128]{2,1,0:T(8,128)(2,1)}, bf16[4,1600,128]{2,1,0:T(8,128)(2,1)}, s32[]{:T(128)}, /...) while((s32[]{:T(128)}, f32[128,8,128]{0,2,1:T(8,128)S(1)}, ...), condition=%wide.region_6.7_spmd, body=%wide.region_5.6_spmd.sunk | while | flops 2112643072 | bytes 33649864 | solution.py:103
  217.9 7.1 %copy.82 = bf16[4,1600,128]{2,0,1:T(4,128)(2,1)S(1)} copy(bf16[4,1600,128]{2,1,0:T(8,128)(2,1)} %get-tuple-element.127) | data formatting | bytes 3276800
  226.8 7.1 %copy.84 = bf16[4,1600,128]{2,0,1:T(4,128)(2,1)S(1)} copy(bf16[4,1600,128]{2,1,0:T(8,128)(2,1)} %get-tuple-element.128) | data formatting | bytes 3276800
  235.4 69.8 %reduce-scatter.7.cloned.1.call-done = bf16[200,512]{1,0:T(8,128)(2,1)} async-done(((bf16[1600,512]{1,0:T(8,128)(2,1)}), bf16[200,512]{1,0:T(8,128)(2,1)}) %reduce-scatter.7.cloned.1.call-update) | async-done | bytes 204816
  306.2 43.9 %reduce-scatter.9.cloned.1.call-done = bf16[200,512]{1,0:T(8,128)(2,1)} async-done(((bf16[1600,512]{1,0:T(8,128)(2,1)}), bf16[200,512]{1,0:T(8,128)(2,1)}) %reduce-scatter.9.cloned.1.call-update) | async-done | bytes 204816
  355.0 11.9 %all-to-all-start.4 = ((bf16[32,200,128]{2,1,0:T(8,128)(2,1)}), bf16[32,200,128]{2,1,0:T(8,128)(2,1)S(1)}, u32[]{:S(2)}, u32[]{:S(2)}) async-start(bf16[32,200,128]{2,1,0:T(8,128)(2,1)} %scatter_fusion.1), calls=%async_computation.4 | async-start | bytes 3276800 | tf_op jit(solution)/shard_map/all_to_all | solution.py:124
  370.8 35.9 %all-to-all-done.4 = bf16[32,200,128]{2,1,0:T(8,128)(2,1)S(1)} async-done(((bf16[32,200,128]{2,1,0:T(8,128)(2,1)}), bf16[32,200,128]{2,1,0:T(8,128)(2,1)S(1)}, u32[]{:S(2)}, u32[]{:S(2)}) %all-to-all-start.4) | async-done | bytes 1638432 | tf_op jit(solution)/shard_map/all_to_all | solution.py:124
  406.7 4.4 all-to-all-start.2
  412.5 38.4 %all-to-all-done.2 = bf16[32,200,128]{2,1,0:T(8,128)(2,1)} async-done(((bf16[32,200,128]{2,1,0:T(8,128)(2,1)}), bf16[32,200,128]{2,1,0:T(8,128)(2,1)}, u32[]{:S(2)}, u32[]{:S(2)}) %all-to-all-start.2) | async-done | bytes 1638432 | tf_op jit(solution)/shard_map/all_to_all | solution.py:117
  450.9 3.9 all-to-all-start.5
  454.8 2.9 copy.73
  457.7 18.8 %all-to-all-done.5 = bf16[32,200,128]{2,0,1:T(8,128)(2,1)S(1)} async-done(((bf16[32,200,128]{2,0,1:T(8,128)(2,1)}), bf16[32,200,128]{2,0,1:T(8,128)(2,1)S(1)}, u32[]{:S(2)}, u32[]{:S(2)}) %all-to-all-start.5) | async-done | bytes 1638432 | tf_op jit(solution)/shard_map/all_to_all | solution.py:123
  476.5 4.6 all-to-all-start.3
  484.5 3.6 reshape.97
  488.1 13.7 %all-to-all-done.3 = bf16[32,200,128]{2,0,1:T(8,128)(2,1)} async-done(((bf16[32,200,128]{2,0,1:T(8,128)(2,1)}), bf16[32,200,128]{2,0,1:T(8,128)(2,1)}, u32[]{:S(2)}, u32[]{:S(2)}) %all-to-all-start.3) | async-done | bytes 1638432 | tf_op jit(solution)/shard_map/all_to_all | solution.py:116
  501.8 3.9 copy.74
  505.7 3.6 reshape.96
  (77 shorter events, 60.2 us)
Async XLA Ops:
  7.2 51.8 %all-gather.5.cloned.1.call-start = ((), (), s32[]{:S(2)}) async-start(), calls=%async_computation.8 | async-start | bytes 1949696 | tf_op jit(solution)/shard_map/all_gather | solution.py:27
  8.8 93.7 %all-gather.9.cloned.1.call-start = ((), (), s32[]{:S(2)}) async-start(), calls=%async_computation.10 | async-start | bytes 1949696 | tf_op jit(solution)/shard_map/all_gather | solution.py:28
  10.4 143.6 %all-gather.11.cloned.1.call-start = ((), (), s32[]{:S(2)}) async-start(), calls=%async_computation.11 | async-start | bytes 1843200 | tf_op jit(solution)/shard_map/all_gather | solution.py:42
  117.9 11.9 %copy-start = (bf16[1,128,1024]{2,1,0:T(8,128)(2,1)S(1)}, bf16[1,128,1024]{2,1,0:T(8,128)(2,1)}, u32[]{:S(2)}) copy-start(bf16[1,128,1024]{2,1,0:T(8,128)(2,1)} %param.13) | copy-start | bytes 786436
  117.9 80.2 %all-gather.7.cloned.1.call-start = ((), (), s32[]{:S(2)}) async-start(), calls=%async_computation.9 | async-start | bytes 1843200 | tf_op jit(solution)/shard_map/all_gather | solution.py:41
  119.4 11.5 %copy-start.1 = (bf16[1,128,1024]{2,1,0:T(8,128)(2,1)S(1)}, bf16[1,128,1024]{2,1,0:T(8,128)(2,1)}, u32[]{:S(2)}) copy-start(bf16[1,128,1024]{2,1,0:T(8,128)(2,1)} %param.12) | copy-start | bytes 786436
  129.8 175.4 %reduce-scatter.7.cloned.1.call-start = ((), (), s32[]{:S(2)}) async-start(), calls=%async_computation.12 | async-start | bytes 1843200
  226.5 123.6 %reduce-scatter.9.cloned.1.call-start = ((), (), s32[]{:S(2)}) async-start(), calls=%async_computation.13 | async-start | bytes 1843200
  233.9 1.5 copy-start.2
  355.0 51.7 %all-to-all-start.4 = ((bf16[32,200,128]{2,1,0:T(8,128)(2,1)}), bf16[32,200,128]{2,1,0:T(8,128)(2,1)S(1)}, u32[]{:S(2)}, u32[]{:S(2)}) async-start(bf16[32,200,128]{2,1,0:T(8,128)(2,1)} %scatter_fusion.1), calls=%async_computation.4 | async-start | bytes 3276800 | tf_op jit(solution)/shard_map/all_to_all | solution.py:124
  406.7 44.2 %all-to-all-start.2 = ((bf16[32,200,128]{2,1,0:T(8,128)(2,1)}), bf16[32,200,128]{2,1,0:T(8,128)(2,1)}, u32[]{:S(2)}, u32[]{:S(2)}) async-start(bf16[32,200,128]{2,1,0:T(8,128)(2,1)} %scatter_fusion), calls=%async_computation.2 | async-start | bytes 3276800 | tf_op jit(solution)/shard_map/all_to_all | solution.py:117
  450.9 25.7 %all-to-all-start.5 = ((bf16[32,200,128]{2,0,1:T(8,128)(2,1)}), bf16[32,200,128]{2,0,1:T(8,128)(2,1)S(1)}, u32[]{:S(2)}, u32[]{:S(2)}) async-start(bf16[32,200,128]{2,0,1:T(8,128)(2,1)} %copy.75), calls=%async_computation.5 | async-start | bytes 3276800 | tf_op jit(solution)/shard_map/all_to_all | solution.py:123
  476.5 25.3 %all-to-all-start.3 = ((bf16[32,200,128]{2,0,1:T(8,128)(2,1)}), bf16[32,200,128]{2,0,1:T(8,128)(2,1)}, u32[]{:S(2)}, u32[]{:S(2)}) async-start(bf16[32,200,128]{2,0,1:T(8,128)(2,1)} %copy.73), calls=%async_computation.3 | async-start | bytes 3276800 | tf_op jit(solution)/shard_map/all_to_all | solution.py:116
Sparse Core Ops, SparseCore 0:
  10.1 48.7 all-gather.4
  61.7 40.8 all-gather.8
  118.0 35.9 all-gather.10
  156.5 41.5 all-gather.6
  226.6 78.5 reduce-scatter.6
  307.9 42.1 reduce-scatter.8
where the time goes:
time: 520 us; the launch traced here: 521 us
  waiting for transfers between devices  372 us (72%)
  local copies, waits for them, and re-layouts  63.8 us (12%)
  starting transfers between devices  25.3 us (5%)
  blocking collectives  16.8 us (3%)
  between operations  16.4 us (3%)
  other arithmetic  12.6 us (2%)
  matrix products  11.4 us (2%)
    unnamed x8, waiting for transfers between devices  114 us
    all_gather x1, waiting for transfers between devices, on_device(): piece_keys = lax.all_gather(image_keys, 'img', axis=0, tiled=True)  46.5 us
    all_gather x1, waiting for transfers between devices, on_device(): piece_values = lax.all_gather(image_values, 'img', axis=0, tiled=True)  41.5 us
    all_gather x1, waiting for transfers between devices, on_device(): lax.all_gather(own_keys, 'seq', axis=1, tiled=True)  41.3 us
    all_to_all x1, waiting for transfers between devices, on_device(): lax.all_to_all(held_keys, 'img', split_axis=0, concat_axis=0, tiled=True)  38.4 us
    all_to_all x1, waiting for transfers between devices, on_device(): lax.all_to_all(held_values, 'img', split_axis=0, concat_axis=0, tiled=True)  35.9 us
    unnamed x20, local copies, waits for them, and re-layouts  27.9 us
    all_gather x1, waiting for transfers between devices, on_device(): lax.all_gather(own_values, 'seq', axis=1, tiled=True)  22 us
  transfers between devices with their start and end apart: 10, of which 10 were waited for; matrix products, arithmetic and copies ran while one was open for 7% of the time, Pallas kernels for 0%

commit v1 on v0

v1 whole, which is shorter than its diff:
```python
import functools
import math

import jax
import jax.numpy as jnp
from jax import lax
from jax.experimental import pallas as pl
from jax.experimental.pallas import tpu as pltpu
from jax.sharding import PartitionSpec as P

MESH = pl.DeviceIdType.MESH
HEAD_DIM = 128
MAX_TILES = 4
GROUP = 8
CORES = 2
SLOT_DEV = 2
BLOCK = 256
FAR = 1e30


def pad16(n):
    return (n + 15) // 16 * 16


def kernel(
    nx, ny, nz,
    q_ref, g_ref, k_ref, v_ref, len_ref, count_ref, slot_ref, gate_ref,
    dq_ref, dk_ref, dv_ref,
    head_out, head_in, tiles, keys, q_cols, g_cols, q_rows, g_rows,
    row_max, row_sum, row_cross, q_acc, terms, y_out, y_in, own,
    mine, twin, z_out, z_in, back_out, back_in,
    send_sem, recv_sem,
):
    tok = k_ref.shape[1]
    part = nx * tok
    rows = dq_ref.shape[1]
    blocks = GROUP * rows // BLOCK
    scale = HEAD_DIM ** -0.5
    img = lax.axis_index("img")
    y = lax.axis_index("seq")
    x = lax.axis_index("head")
    z, core = img // CORES, img % CORES

    def at_z(t):
        return {"img": lax.rem(z + (t + nz), nz) * CORES + core}

    def at_y(t):
        return {"seq": lax.rem(y + (t + ny), ny)}

    def at_x(t):
        return {"head": lax.rem(x + (t + nx), nx)}

    other_core = {"img": z * CORES + (1 - core)}

    partners = [at_x(t) for t in range(1, nx)] + [other_core]
    for n, at in ((nz, at_z), (ny, at_y)):
        partners += [at(1), at(-1)] if n > 2 else [at(1)]
    barrier = pltpu.get_barrier_semaphore()
    for device in partners:
        pl.semaphore_signal(barrier, inc=1, device_id=device, device_id_type=MESH)

    started = []

    def send(src, dst, device):
        index = len(started)
        copy = pltpu.make_async_remote_copy(
            src_ref=src, dst_ref=dst, send_sem=send_sem.at[index], recv_sem=recv_sem.at[index],
            device_id=device, device_id_type=MESH,
        )
        copy.start()
        started.append(copy)
        return copy

    for h in range(nx):
        for s in range(SLOT_DEV):
            for kv, ref in enumerate((k_ref, v_ref)):
                head_out[h, 2 * s + kv, 0:tok, :] = ref[s, :, h * HEAD_DIM:(h + 1) * HEAD_DIM]
    pl.semaphore_wait(barrier, len(partners))
    arriving = [
        send(head_out.at[lax.rem(x + t, nx)], head_in.at[t], at_x(t)) for t in range(1, nx)
    ]

    positions = y * rows + lax.broadcasted_iota(jnp.int32, (rows, HEAD_DIM), 0)
    live = positions < len_ref[0]
    for g in range(GROUP):
        cut = slice(g * HEAD_DIM, (g + 1) * HEAD_DIM)
        b, r = g * rows // BLOCK, g * rows % BLOCK
        query = q_ref[0, :, cut]
        grad = jnp.where(live, g_ref[0, :, cut], jnp.zeros((rows, HEAD_DIM), jnp.bfloat16))
        q_rows[b, r:r + rows, :] = query
        g_rows[b, r:r + rows, :] = grad
        q_cols[b, :, r:r + rows] = query.T
        g_cols[b, :, r:r + rows] = grad.T
    row_max[...] = jnp.full(row_max.shape, -FAR, jnp.float32)
    row_sum[...] = jnp.zeros(row_sum.shape, jnp.float32)
    row_cross[...] = jnp.zeros(row_cross.shape, jnp.float32)
    q_acc[...] = jnp.zeros(q_acc.shape, jnp.float32)

    for t in range(nx):
        if t > 0:
            arriving[t - 1].wait_recv()
        for q in range(2 * SLOT_DEV):
            block = head_out[x, q, 0:tok, :] if t == 0 else head_in[t, q, 0:tok, :]
            tiles[0, 0, q // 2, q % 2, t * tok:(t + 1) * tok, :] = block

    def gather(n, at, ref, halves, forward=None, work=None):
        half = n // 2
        right = left = None
        if forward is not None:
            forward(0)
        for t in range(1, half + 1):
            if right is not None:
                right.wait_recv()
            if t < half:
                next_right = send(ref(-(t - 1) % n), ref(-t % n), at(1))
            else:
                next_right = send(halves(-(t - 1) % n, 0), halves(half, 0), at(1))
            if left is not None:
                left.wait_recv()
            if t < half:
                next_left = send(ref(t - 1), ref(t), at(-1))
            else:
                next_left = send(halves(t - 1, 1), halves(half, 1), at(-1))
            if forward is not None and t > 1:
                forward(-(t - 1) % n)
                forward(t - 1)
            if work is not None:
                work([0] if t == 1 else [t - 1, -(t - 1) % n])
            right, left = next_right, next_left
        right.wait_recv()
        left.wait_recv()
        if forward is not None:
            forward(half)
        if work is not None:
            work([half])

    twins = []
    gather(
        nz, at_z, lambda d: tiles.at[d, 0], lambda d, p: tiles.at[d, 0, p],
        forward=lambda d: twins.append(send(tiles.at[d, 0], tiles.at[d, 1], other_core)),
    )
    for copy in twins:
        copy.wait_recv()

    for j in range(MAX_TILES):
        slot = jnp.maximum(slot_ref[0, j], 0)
        owner = slot // SLOT_DEV
        step = (owner // CORES + (nz - z)) % nz
        side = (owner + core) % CORES
        for kv in range(2):
            keys[0, kv, j * part:(j + 1) * part, :] = (
                tiles[step, side, slot % SLOT_DEV, kv][0:part]
            )

    bias = [jnp.where(j < count_ref[0], 0.0, FAR).astype(jnp.float32) for j in range(MAX_TILES)]
    to_exp2 = scale * math.log2(math.e)

    def scores_of(c, b):
        scores = jnp.dot(keys[c, 0], q_cols[b], preferred_element_type=jnp.float32) * to_exp2
        grads = jnp.dot(keys[c, 1], g_cols[b], preferred_element_type=jnp.float32)
        return scores, grads

    def tile_rows(j):
        return slice(j * part, (j + 1) * part)

    def first_sweep(chunks):
        def body(i, carry):
            b = i % blocks
            c = chunks[0] if len(chunks) == 1 else jnp.where(i < blocks, chunks[0], chunks[1])
            scores, grads = scores_of(c, b)
            old = row_max[b]
            top = old
            for j in range(MAX_TILES):
                highest = jnp.max(scores[tile_rows(j)], axis=0, keepdims=True)
                top = jnp.maximum(top, highest - bias[j])
            shrink = jnp.exp2(old - top)
            total = row_sum[b] * shrink
            cross = row_cross[b] * shrink
            for j in range(MAX_TILES):
                e = jnp.exp2(scores[tile_rows(j)] - (top + bias[j]))
                total = total + jnp.sum(e, axis=0, keepdims=True)
                cross = cross + jnp.sum(e * grads[tile_rows(j)], axis=0, keepdims=True)
            row_max[b] = top
            row_sum[b] = total
            row_cross[b] = cross
            return carry

        lax.fori_loop(0, len(chunks) * blocks, body, 0)

    gather(
        ny, at_y, lambda d: keys.at[d], lambda d, p: keys.at[d, p], work=first_sweep
    )
    row_max[...] = row_max[...] + jnp.log2(row_sum[...])
    row_cross[...] = row_cross[...] / row_sum[...]

    gate = jnp.tanh(jnp.full((8, HEAD_DIM), gate_ref[0], jnp.float32))[0:1]
    grad_factor = gate * scale

    def second_sweep(chunks):
        for i in range(len(chunks)):
            terms[i] = jnp.zeros(terms.shape[1:], jnp.float32)

        def body(i, carry):
            b = i % blocks
            if len(chunks) == 1:
                c, w = chunks[0], 0
            else:
                c, w = jnp.where(i < blocks, chunks[0], chunks[1]), i // blocks
            scores, grads = scores_of(c, b)
            top, delta = row_max[b], row_cross[b]
            weights, score_grads = [], []
            for j in range(MAX_TILES):
                p = jnp.exp2(scores[tile_rows(j)] - (top + bias[j]))
                weights.append(p)
                score_grads.append(p * (grads[tile_rows(j)] - delta))
            weights = jnp.concatenate(weights, axis=0).astype(jnp.bfloat16)
            score_grads = jnp.concatenate(score_grads, axis=0).astype(jnp.bfloat16)
            terms[w, 0] += jnp.dot(score_grads, q_rows[b], preferred_element_type=jnp.float32)
            terms[w, 1] += jnp.dot(weights, g_rows[b], preferred_element_type=jnp.float32)
            q_acc[b] += lax.dot_general(
                score_grads, keys[c, 0], (((0,), (0,)), ((), ())),
                preferred_element_type=jnp.float32,
            )
            return carry

        lax.fori_loop(0, len(chunks) * blocks, body, 0)

    def scatter(n, at, block, out, arrived, prepare):
        half = n // 2
        right = left = None
        for s in range(half):
            t = half - s
            if s == 0:
                prepare([half])
                out[0, 0, 0] = block(0, half, 0)
                out[1, 0, 1] = block(0, half, 1)
                right = send(out.at[0, 0, 0], arrived.at[0, 0, 0], at(1))
                left = send(out.at[1, 0, 1], arrived.at[1, 0, 1], at(-1))
                continue
            prepare([t, n - t])
            for way in range(2):
                (right, left)[way].wait_recv()
                for p in range(2):
                    value = block(way, (t, n - t)[way], p)
                    if s > 1 or p == way:
                        value = value + arrived[way, s - 1, p]
                    out[way, s, p] = value.astype(out.dtype)
                copy = send(out.at[way, s], arrived.at[way, s], at((1, -1)[way]))
                if way == 0:
                    right = copy
                else:
                    left = copy
        prepare([0])
        right.wait_recv()
        left.wait_recv()
        totals = []
        for p in range(2):
            value = block(0, 0, p)
            for way in range(2):
                if half > 1 or p == way:
                    value = value + arrived[way, half - 1, p]
            totals.append(value)
        return totals

    def y_block(w, d, p):
        value = terms[w, p] * (grad_factor if p == 0 else gate)
        return value

    def y_start(w, d, p):
        return y_block(w, d, p)

    sums = scatter(
        ny, at_y, lambda w, d, p: y_block(w, d, p).astype(jnp.bfloat16)
        if d == ny // 2 else y_block(w, d, p),
        y_out, y_in, second_sweep,
    )
    for kv in range(2):
        for j in range(MAX_TILES):
            own[j, kv, 0:part, :] = sums[kv][j * part:(j + 1) * part].astype(jnp.bfloat16)

    def build(d, side):
        for s in range(SLOT_DEV):
            slot = ((z + d) % nz * CORES + (core + side) % CORES) * SLOT_DEV + s
            which = 0
            found = 0
            for j in range(MAX_TILES):
                hit = jnp.where((slot_ref[0, j] == slot) & (j < count_ref[0]), 1, 0)
                which = which + hit * j
                found = found + hit
            for kv in range(2):
                block = own[which, kv]
                mine[d, side, s, kv] = jnp.where(found > 0, block, jnp.zeros_like(block))

    order = [nz // 2]
    for t in range(nz // 2 - 1, 0, -1):
        order += [t, nz - t]
    order += [0]
    from_twin = {}
    for d in order:
        build(d, 1)
        from_twin[d] = send(mine.at[d, 1], twin.at[d], other_core)
    for d in order:
        build(d, 0)

    for g in range(GROUP):
        b, r = g * rows // BLOCK, g * rows % BLOCK
        dq_ref[0, :, g * HEAD_DIM:(g + 1) * HEAD_DIM] = (
            q_acc[b, r:r + rows, :] * grad_factor
        ).astype(jnp.bfloat16)

    def z_prepare(places):
        for d in places:
            from_twin[d].wait_recv()

    slots = scatter(
        nz, at_z, lambda w, d, p: mine[d, 0, p] + twin[d, p], z_out, z_in, z_prepare
    )

    for s in range(SLOT_DEV):
        for kv in range(2):
            value = slots[s][kv]
            for t in range(nx):
                back_out[t, 2 * s + kv, 0:tok, :] = value[t * tok:(t + 1) * tok]
    returns = [send(back_out.at[t], back_in.at[x], at_x(-t)) for t in range(1, nx)]
    back_in[x] = back_out[0]
    for copy in returns:
        copy.wait_recv()
    for h in range(nx):
        for s in range(SLOT_DEV):
            for kv, ref in enumerate((dk_ref, dv_ref)):
                ref[s, :, h * HEAD_DIM:(h + 1) * HEAD_DIM] = back_in[h, 2 * s + kv, 0:tok, :]
    for copy in started:
        copy.wait_send()


def on_device(mesh_sizes, queries, out_grad, text_len, image_keys, image_values, tile_counts,
              tile_slots, gate_param):
    nx, ny, nz = mesh_sizes
    tok = image_keys.shape[1]
    rows = queries.shape[1]
    part = nx * tok
    pad, tok_pad = pad16(part), pad16(tok)
    span = MAX_TILES * part
    blocks = GROUP * rows // BLOCK
    bf16, f32 = jnp.bfloat16, jnp.float32
    vmem = pl.BlockSpec(memory_space=pltpu.VMEM)
    smem = pl.BlockSpec(memory_space=pltpu.SMEM)
    d = HEAD_DIM
    scratch = [
        ((nx, 2 * SLOT_DEV, tok_pad, d), bf16),
        ((nx, 2 * SLOT_DEV, tok_pad, d), bf16),
        ((nz, CORES, SLOT_DEV, 2, pad, d), bf16),
        ((ny, 2, span, d), bf16),
        ((blocks, d, BLOCK), bf16),
        ((blocks, d, BLOCK), bf16),
        ((blocks, BLOCK, d), bf16),
        ((blocks, BLOCK, d), bf16),
        ((blocks, 1, BLOCK), f32),
        ((blocks, 1, BLOCK), f32),
        ((blocks, 1, BLOCK), f32),
        ((blocks, BLOCK, d), f32),
        ((2, 2, span, d), f32),
        ((2, ny // 2, 2, span, d), bf16),
        ((2, ny // 2, 2, span, d), bf16),
        ((MAX_TILES, 2, pad, d), bf16),
        ((nz, CORES, SLOT_DEV, 2, pad, d), bf16),
        ((nz, SLOT_DEV, 2, pad, d), bf16),
        ((2, nz // 2, SLOT_DEV, 2, pad, d), bf16),
        ((2, nz // 2, SLOT_DEV, 2, pad, d), bf16),
        ((nx, 2 * SLOT_DEV, tok_pad, d), bf16),
        ((nx, 2 * SLOT_DEV, tok_pad, d), bf16),
    ]
    copies = 2 * (nx - 1) + 2 * (ny + ny) + 2 * (nz + nz) + 2 * nz
    return pl.pallas_call(
        functools.partial(kernel, nx, ny, nz),
        out_shape=(
            jax.ShapeDtypeStruct(queries.shape, bf16),
            jax.ShapeDtypeStruct(image_keys.shape, bf16),
            jax.ShapeDtypeStruct(image_values.shape, bf16),
        ),
        in_specs=[vmem, vmem, vmem, vmem, smem, smem, smem, smem],
        out_specs=(vmem, vmem, vmem),
        scratch_shapes=[pltpu.VMEM(shape, dtype) for shape, dtype in scratch] + [
            pltpu.SemaphoreType.DMA((copies,)),
            pltpu.SemaphoreType.DMA((copies,)),
        ],
        compiler_params=pltpu.CompilerParams(
            collective_id=0, has_side_effects=True, vmem_limit_bytes=56 * 1024 * 1024
        ),
        name="cross_attention_backward",
    )(queries, out_grad, image_keys, image_values, text_len, tile_counts, tile_slots, gate_param)


def solution(mesh):
    sizes = (mesh.shape["head"], mesh.shape["seq"], mesh.shape["img"] // CORES)
    return jax.shard_map(
        functools.partial(on_device, sizes),
        mesh=mesh,
        in_specs=(
            P("img", "seq", "head"),
            P("img", "seq", "head"),
            P("img"),
            P("img", ("seq", "head"), None),
            P("img", ("seq", "head"), None),
            P("img"),
            P("img", None),
            P(),
        ),
        out_specs=(
            P("img", "seq", "head"),
            P("img", ("seq", "head"), None),
            P("img", ("seq", "head"), None),
        ),
        check_vma=False,
    )
```

time: 520 us -> 160 us (0.31)
  waiting for transfers between devices: 372 us -> 0 us
  Pallas kernels: 0 us -> 150 us
  local copies, waits for them, and re-layouts: 63.8 us -> 6.24 us
  starting transfers between devices: 25.3 us -> 0 us
  blocking collectives: 16.8 us -> 0 us
  between operations: 16.4 us -> 2.6 us
  other arithmetic: 12.6 us -> 0 us
  matrix products: 11.4 us -> 0 us
    all_gather x4 -> x0, waiting for transfers between devices: 151 us -> none  [the longest x1 46.5 us: on_device(): piece_keys = lax.all_gather(image_keys, 'img', axis=0, tiled=True)]
    pallas_call x0 -> x1, Pallas kernels: none -> 150 us  [on_device(): pl.pallas_call(functools.partial(kernel, nx, ny, nz), out_shape=(jax.Shap...]
    unnamed x8 -> x0, waiting for transfers between devices: 114 us -> none
    all_to_all x4 -> x0, waiting for transfers between devices: 107 us -> none  [the longest x1 38.4 us: on_device(): lax.all_to_all(held_keys, 'img', split_axis=0, concat_axis=0, tiled=True)]
    unnamed x20 -> x7, local copies, waits for them, and re-layouts: 27.9 us -> 2.96 us
    all_to_all x4 -> x0, starting transfers between devices: 24.8 us -> none  [the longest x1 11.9 us: on_device(): lax.all_to_all(held_values, 'img', split_axis=0, concat_axis=0, tiled=True)]
    all_to_all x2 -> x0, blocking collectives: 16.8 us -> none  [the longest x1 9.1 us: on_device(): lax.all_to_all(own_values, 'head', split_axis=2, concat_axis=1, tiled=True)]
    all_to_all x6 -> x0, local copies, waits for them, and re-layouts: 12.6 us -> none  [the longest x1 3.88 us: on_device(): lax.all_to_all(lax.all_to_all(held_keys, 'img', split_axis=0, concat_axis...]
  transfers between devices with their start and end apart: 10 -> 0, of which waited for: 10 -> 0; matrix products, arithmetic and copies ran while one was open for 7% -> 0% of each run, Pallas kernels for 0% -> 0%
where the time goes in v1:
time: 160 us; the launch traced here: 158 us
  Pallas kernels  150 us (94%)
  local copies, waits for them, and re-layouts  6.24 us (4%)
  between operations  2.6 us (2%)
    pallas_call x1, Pallas kernels, on_device(): pl.pallas_call(functools.partial(kernel, nx, ny, nz), out_shape=(jax.Shap...  150 us
    pallas_call x2, local copies, waits for them, and re-layouts, on_device(): pl.pallas_call(functools.partial(kernel, nx, ny, nz), out_shape=(jax.Shap...  3.28 us

profile of v1, /device:TPU:1, one launch (start us, length us, event | category | flops | bytes accessed | tf_op | source)
XLA Modules:
  0.0 158.4 jit_solution(10905474624620463866)
XLA Ops:
  2.6 0.0 copy-start.1
  2.6 1.6 %copy.11.k_ref = bf16[2,50,512]{2,1,0:T(8,128)(2,1)} copy(bf16[2,50,512]{2,0,1:T(2,128)(2,1)} %param.11) | data formatting | bytes 204800 | tf_op args[3]
  4.2 0.0 copy-done.1
  4.2 0.7 copy.12.v_ref
  4.8 149.6 %cross_attention_backward.1 = (bf16[1,128,1024]{2,1,0:T(8,128)(2,1)}, bf16[2,50,512]{2,1,0:T(8,128)(2,1)}, bf16[2,50,512]{2,1,0:T(8,128)(2,1)}) custom-call(bf16[1,128,1024]{2,1,0:T(8,128)(2,1)} %q_ref.1, bf16[1,128,1024]{2,1,0:T(8,128)(2,1)} %g_ref.1, bf16[2,50,512]{2,1,0:T(8,128)(2,1)} %copy.11.k_ref, bf16[2,50,512]{2,1,0:T(8,128)(2,1)} %copy.12.v_ref, ...), custom_call_target="tpu_custom_call" | custom-call | tf_op jit(solution)/shard_map/cross_attention_backward/pallas_call | solution.py:374
  154.4 0.0 copy-start
  154.4 1.7 %copy.13 = bf16[2,50,512]{2,0,1:T(2,128)(2,1)} copy(bf16[2,50,512]{2,1,0:T(8,128)(2,1)} %get-tuple-element.4) | data formatting | bytes 204800 | tf_op jit(solution)/shard_map/cross_attention_backward/pallas_call | solution.py:374
  156.1 1.6 %copy.14 = bf16[2,50,512]{2,0,1:T(2,128)(2,1)} copy(bf16[2,50,512]{2,1,0:T(8,128)(2,1)} %get-tuple-element.5) | data formatting | bytes 204800 | tf_op jit(solution)/shard_map/cross_attention_backward/pallas_call | solution.py:374
  157.7 0.0 copy-done
  157.7 0.7 copy.19
Async XLA Ops:
  2.6 1.6 %copy-start.1 = (bf16[2,50,512]{2,0,1:T(2,128)(2,1)S(1)}, bf16[2,50,512]{2,0,1:T(2,128)(2,1)}, u32[]{:S(2)}) copy-start(bf16[2,50,512]{2,0,1:T(2,128)(2,1)} %param.12) | copy-start | bytes 307204
  154.4 3.3 %copy-start = (bf16[1,128,1024]{2,1,0:T(8,128)(2,1)S(1)}, bf16[1,128,1024]{2,1,0:T(8,128)(2,1)}, u32[]{:S(2)}) copy-start(bf16[1,128,1024]{2,1,0:T(8,128)(2,1)} %get-tuple-element.9) | copy-start | bytes 786436

commit v2 on v1

v2 whole, which is shorter than its diff:
```python
import functools
import math

import jax
import jax.numpy as jnp
from jax import lax
from jax.experimental import pallas as pl
from jax.experimental.pallas import tpu as pltpu
from jax.sharding import PartitionSpec as P

MESH = pl.DeviceIdType.MESH
HEAD_DIM = 128
MAX_TILES = 4
GROUP = 8
CORES = 2
SLOT_DEV = 2
BLOCK = 256
FAR = 1e30


def pad16(n):
    return (n + 15) // 16 * 16


def kernel(
    nx, ny, nz,
    q_hbm, g_hbm, k_hbm, v_hbm, len_ref, count_ref, slot_ref, gate_ref,
    dq_hbm, dk_ref, dv_ref,
    q_ref, g_ref, k_ref, v_ref, dq_ref, head_out, head_in, tiles, keys, rowed,
    stat_out, stat_in, final, terms, q_terms, q_own, y_out, y_in, own,
    mine, twin, z_out, z_in, back_out, back_in,
    send_sem, recv_sem, local_sem,
):
    tok = k_ref.shape[0]
    part = nx * tok
    rows = q_ref.shape[1]
    blocks = GROUP * rows // BLOCK
    scale = HEAD_DIM ** -0.5
    img = lax.axis_index("img")
    y = lax.axis_index("seq")
    x = lax.axis_index("head")
    z, core = img // CORES, img % CORES

    def at_z(t):
        return {"img": lax.rem(z + (t + nz), nz) * CORES + core}

    def at_y(t):
        return {"seq": lax.rem(y + (t + ny), ny)}

    def at_x(t):
        return {"head": lax.rem(x + (t + nx), nx)}

    other_core = {"img": z * CORES + (1 - core)}

    loads = []
    for i, (src, dst) in enumerate(
        ((k_hbm, k_ref), (v_hbm, v_ref), (q_hbm, q_ref), (g_hbm, g_ref))
    ):
        loads.append(pltpu.make_async_copy(src, dst, local_sem.at[i]))
        loads[i].start()

    partners = [at_x(t) for t in range(1, nx)] + [other_core]
    partners += [at_y(t) for t in range(1, ny)]
    partners += [at_z(1), at_z(-1)] if nz > 2 else [at_z(1)]
    barrier = pltpu.get_barrier_semaphore()
    for device in partners:
        pl.semaphore_signal(barrier, inc=1, device_id=device, device_id_type=MESH)

    started = []

    def send(src, dst, device):
        index = len(started)
        copy = pltpu.make_async_remote_copy(
            src_ref=src, dst_ref=dst, send_sem=send_sem.at[index], recv_sem=recv_sem.at[index],
            device_id=device, device_id_type=MESH,
        )
        copy.start()
        started.append(copy)
        return copy

    def run(steps, *rings):
        for _ in range(steps):
            for ring in rings:
                next(ring, None)

    for kv, ref in enumerate((k_ref, v_ref)):
        loads[kv].wait()
        for h in range(nx):
            both = ref[:, :, h * HEAD_DIM:(h + 1) * HEAD_DIM].astype(jnp.float32)
            for s in range(SLOT_DEV):
                head_out[h, 2 * s + kv, 0:tok, :] = both[:, s, :].astype(jnp.bfloat16)
    pl.semaphore_wait(barrier, len(partners))
    arriving = {}
    for t in sorted(range(1, nx), key=lambda t: min(t, nx - t)):
        arriving[t] = send(head_out.at[lax.rem(x + t, nx)], head_in.at[t], at_x(t))

    live = y * rows + lax.broadcasted_iota(jnp.int32, (rows, HEAD_DIM), 0) < len_ref[0]
    loads[2].wait()
    loads[3].wait()
    for g in range(GROUP):
        cut = slice(g * HEAD_DIM, (g + 1) * HEAD_DIM)
        b, r = g * rows // BLOCK, g * rows % BLOCK
        rowed[0, 0, b, r:r + rows, :] = q_ref[0, :, cut]
        rowed[0, 1, b, r:r + rows, :] = jnp.where(
            live, g_ref[0, :, cut], jnp.zeros((rows, HEAD_DIM), jnp.bfloat16)
        )

    def gather(n, at, ref):
        half = n // 2
        copies = {}
        for t in range(1, half + 1):
            for h in range(2):
                for way, step in enumerate((1, -1)):
                    if (way, h) in copies:
                        copies.pop((way, h)).wait_recv()
                    if t < half or h == way:
                        source, target = ref(-step * (t - 1) % n, h), ref(-step * t % n, h)
                        copies[way, h] = send(source, target, at(step))
                yield
        for copy in copies.values():
            copy.wait_recv()
        yield

    def collect():
        for t in range(nx):
            if t > 0:
                arriving[t].wait_recv()
            for q in range(2 * SLOT_DEV):
                block = head_out[x, q, 0:tok, :] if t == 0 else head_in[t, q, 0:tok, :]
                tiles[0, 0, q // 2, q % 2, t * tok:(t + 1) * tok, :] = block

    def gather_z():
        ring = gather(nz, at_z, lambda d, h: tiles.at[d, 0, h])
        twins = []

        def forward(d):
            twins.append(send(tiles.at[d, 0], tiles.at[d, 1], other_core))

        for t in range(1, nz // 2 + 1):
            next(ring)
            next(ring)
            for d in [0] if t == 1 else [t - 1, -(t - 1) % nz]:
                forward(d)
            yield
        next(ring)
        forward(nz // 2)
        yield
        for copy in twins:
            copy.wait_recv()
        for j in range(MAX_TILES):
            slot = jnp.maximum(slot_ref[0, j], 0)
            owner = slot // SLOT_DEV
            step = (owner // CORES + (nz - z)) % nz
            side = (owner + core) % CORES
            for kv in range(2):
                keys[kv, tile_rows(j), :] = tiles[step, side, slot % SLOT_DEV, kv][0:part]
        yield

    bias = [jnp.where(j < count_ref[0], 0.0, FAR).astype(jnp.float32) for j in range(MAX_TILES)]
    to_exp2 = scale * math.log2(math.e)
    by_columns = (((1,), (1,)), ((), ()))

    def scores_of(c, b):
        scores = lax.dot_general(
            keys[0], rowed[c, 0, b], by_columns, preferred_element_type=jnp.float32
        ) * to_exp2
        grads = lax.dot_general(
            keys[1], rowed[c, 1, b], by_columns, preferred_element_type=jnp.float32
        )
        return scores, grads

    def tile_rows(j):
        return slice(j * part, (j + 1) * part)

    def over(chunks, body):
        def step(i, carry):
            if len(chunks) == 1:
                body(chunks[0], 0, i)
            else:
                body(jnp.where(i < blocks, chunks[0], chunks[1]), i // blocks, i % blocks)
            return carry

        lax.fori_loop(0, len(chunks) * blocks, step, 0)

    stats = {}

    def first_sweep(chunks):
        def body(c, w, b):
            scores, grads = scores_of(c, b)
            top = jnp.full((1, BLOCK), -FAR, jnp.float32)
            for j in range(MAX_TILES):
                highest = jnp.max(scores[tile_rows(j)], axis=0, keepdims=True)
                top = jnp.maximum(top, highest - bias[j])
            total = jnp.zeros((1, BLOCK), jnp.float32)
            cross = jnp.zeros((1, BLOCK), jnp.float32)
            for j in range(MAX_TILES):
                e = jnp.exp2(scores[tile_rows(j)] - (top + bias[j]))
                total = total + jnp.sum(e, axis=0, keepdims=True)
                cross = cross + jnp.sum(e * grads[tile_rows(j)], axis=0, keepdims=True)
            stat_out[c, 0, b] = top
            stat_out[c, 1, b] = total
            stat_out[c, 2, b] = cross

        over(chunks, body)
        for d in chunks:
            if d != 0:
                stats[d] = send(stat_out.at[d], stat_in.at[(ny - d) % ny], at_y(d))

    gate = jnp.tanh(jnp.full((8, HEAD_DIM), gate_ref[0], jnp.float32))[0:1]
    grad_factor = gate * scale

    def second_sweep(chunks):
        def body(c, w, b):
            scores, grads = scores_of(c, b)
            top, delta = final[c, 0, b], final[c, 1, b]
            weights, score_grads = [], []
            for j in range(MAX_TILES):
                e = jnp.exp2(scores[tile_rows(j)] - (top + bias[j]))
                weights.append(e)
                score_grads.append(e * (grads[tile_rows(j)] - delta))
            weights = jnp.concatenate(weights, axis=0).astype(jnp.bfloat16)
            score_grads = jnp.concatenate(score_grads, axis=0).astype(jnp.bfloat16)
            terms[0] += jnp.dot(score_grads, rowed[c, 0, b], preferred_element_type=jnp.float32)
            terms[1] += jnp.dot(weights, rowed[c, 1, b], preferred_element_type=jnp.float32)
            q_terms[w, b] = lax.dot_general(
                score_grads, keys[0], (((0,), (0,)), ((), ())),
                preferred_element_type=jnp.float32,
            )

        over(chunks, body)

    def scatter(n, at, block, out, arrived, prepare, finish):
        half = n // 2
        copies = {}

        def total(value, h, step):
            for way in range(2) if step == 0 else [0 if step > 0 else 1]:
                if (way, h) in copies:
                    copies.pop((way, h)).wait_recv()
                    value = value + arrived[way, half - abs(step) - 1, h]
            return value

        for s in range(half):
            t = half - s
            prepare([half] if s == 0 else [t, n - t])
            for h in range(2):
                for way, step in enumerate((1, -1)):
                    if s == 0 and h != way:
                        continue
                    value = block(way if s > 0 else 0, step * t % n, h)
                    out[way, s, h] = total(value, h, step * t).astype(out.dtype)
                    copies[way, h] = send(out.at[way, s, h], arrived.at[way, s, h], at(step))
            yield
        prepare([0])
        for h in range(2):
            finish(h, total(block(0, 0, h), h, 0))
        yield

    half_blocks = blocks // 2

    def query_block(w, d, h):
        cut = slice(h * half_blocks, (h + 1) * half_blocks)
        return q_own[cut] if d == 0 else q_terms[w, cut]

    def query_finish(h, value):
        value = value * grad_factor[None]
        for i in range(half_blocks):
            for r in range(0, BLOCK, rows):
                g = ((h * half_blocks + i) * BLOCK + r) // rows
                dq_ref[0, :, g * HEAD_DIM:(g + 1) * HEAD_DIM] = (
                    value[i, r:r + rows].astype(jnp.bfloat16)
                )

    def build(d, side):
        for s in range(SLOT_DEV):
            slot = ((z + d) % nz * CORES + (core + side) % CORES) * SLOT_DEV + s
            which = 0
            found = 0
            for j in range(MAX_TILES):
                hit = jnp.where((slot_ref[0, j] == slot) & (j < count_ref[0]), 1, 0)
                which = which + hit * j
                found = found + hit
            for kv in range(2):
                block = own[which, kv]
                mine[d, side, s, kv] = jnp.where(found > 0, block, jnp.zeros_like(block))

    def scatter_z():
        for kv in range(2):
            value = terms[kv] * (gate if kv else grad_factor)
            for j in range(MAX_TILES):
                own[j, kv, 0:part, :] = value[tile_rows(j)].astype(jnp.bfloat16)
        order = [nz // 2]
        for t in range(nz // 2 - 1, 0, -1):
            order += [t, nz - t]
        order += [0]
        from_twin = {}
        for d in order:
            build(d, 1)
            from_twin[d] = send(mine.at[d, 1], twin.at[d], other_core)
        for d in order:
            build(d, 0)
        yield

        def prepare(places):
            for d in places:
                from_twin[d].wait_recv()

        def finish(s, value):
            for kv in range(2):
                for t in range(nx):
                    back_out[t, 2 * s + kv, 0:tok, :] = value[kv, t * tok:(t + 1) * tok]

        yield from scatter(
            nz, at_z, lambda w, d, s: mine[d, 0, s] + twin[d, s], z_out, z_in, prepare, finish
        )

    z_half, y_half = nz // 2, ny // 2
    y_ring = gather(ny, at_y, lambda d, h: rowed.at[d, h])
    z_ring = gather_z()
    run(2, y_ring)
    collect()
    run(1, z_ring)
    terms[...] = jnp.zeros(terms.shape, jnp.float32)
    y_steps = 2
    for step in range(z_half):
        if y_steps < 2 * y_half - 2:
            run(1, y_ring)
            y_steps += 1
        run(1, z_ring)
    run(1, z_ring)
    swept = 0
    while y_steps <= 2 * y_half:
        arrived = (y_steps - 2) // 2 if y_steps <= 2 * y_half else y_half
        first_sweep([0] if swept == 0 else [swept, ny - swept])
        swept += 1
        while y_steps <= 2 * y_half and (y_steps - 2) // 2 < swept:
            run(1, y_ring)
            y_steps += 1
    while swept < y_half:
        first_sweep([swept, ny - swept])
        swept += 1
    first_sweep([y_half])

    stat_in[0] = stat_out[0]
    order = sorted(range(1, ny), key=lambda d: -min(d, ny - d))
    for d in order:
        stats[d].wait_recv()
    top = stat_in[0, 0]
    for d in range(1, ny):
        top = jnp.maximum(top, stat_in[d, 0])
    total = jnp.zeros_like(top)
    cross = jnp.zeros_like(top)
    for d in range(ny):
        shrink = jnp.exp2(stat_in[d, 0] - top)
        total = total + stat_in[d, 1] * shrink
        cross = cross + stat_in[d, 2] * shrink
    final[0, 0] = top + jnp.log2(total)
    final[0, 1] = cross / total
    finals = {d: send(final.at[0], final.at[(ny - d) % ny], at_y(d)) for d in order}

    def query_prepare(places):
        for d in places:
            if d != 0:
                finals[(ny - d) % ny].wait_recv()
        if places != [0]:
            second_sweep(places)

    second_sweep([0])
    q_own[...] = q_terms[0]
    y_ring = scatter(ny, at_y, query_block, y_out, y_in, query_prepare, query_finish)
    run(y_half, y_ring)
    z_ring = scatter_z()
    run(3, z_ring)
    run(1, y_ring)
    store = pltpu.make_async_copy(dq_ref, dq_hbm, local_sem.at[0])
    store.start()
    run(z_half, z_ring)

    returns = [send(back_out.at[t], back_in.at[x], at_x(-t)) for t in range(1, nx)]
    back_in[x] = back_out[0]
    for copy in returns:
        copy.wait_recv()
    for h in range(nx):
        for kv, ref in enumerate((dk_ref, dv_ref)):
            both = [
                back_in[h, 2 * s + kv, 0:tok, :].astype(jnp.float32) for s in range(SLOT_DEV)
            ]
            ref[:, :, h * HEAD_DIM:(h + 1) * HEAD_DIM] = (
                jnp.stack(both, axis=1).astype(jnp.bfloat16)
            )
    for copy in started:
        copy.wait_send()
    store.wait()


def on_device(mesh_sizes, queries, out_grad, text_len, image_keys, image_values, tile_counts,
              tile_slots, gate_param):
    nx, ny, nz = mesh_sizes
    tok = image_keys.shape[1]
    rows = queries.shape[1]
    part = nx * tok
    tok_pad = pad16(tok)
    image_keys = jnp.transpose(image_keys, (1, 0, 2))
    image_values = jnp.transpose(image_values, (1, 0, 2))
    pad = pad16(part)
    span = MAX_TILES * part
    blocks = GROUP * rows // BLOCK
    bf16, f32 = jnp.bfloat16, jnp.float32
    vmem = pl.BlockSpec(memory_space=pltpu.VMEM)
    smem = pl.BlockSpec(memory_space=pltpu.SMEM)
    hbm = pl.BlockSpec(memory_space=pl.ANY)
    d = HEAD_DIM
    scratch = [
        (queries.shape, bf16),
        (queries.shape, bf16),
        (image_keys.shape, bf16),
        (image_keys.shape, bf16),
        (queries.shape, bf16),
        ((nx, 2 * SLOT_DEV, tok_pad, d), bf16),
        ((nx, 2 * SLOT_DEV, tok_pad, d), bf16),
        ((nz, CORES, SLOT_DEV, 2, pad, d), bf16),
        ((2, span, d), bf16),
        ((ny, 2, blocks, BLOCK, d), bf16),
        ((ny, 3, blocks, 1, BLOCK), f32),
        ((ny, 3, blocks, 1, BLOCK), f32),
        ((ny, 2, blocks, 1, BLOCK), f32),
        ((2, span, d), f32),
        ((2, blocks, BLOCK, d), f32),
        ((blocks, BLOCK, d), f32),
        ((2, ny // 2, 2, blocks // 2, BLOCK, d), bf16),
        ((2, ny // 2, 2, blocks // 2, BLOCK, d), bf16),
        ((MAX_TILES, 2, pad, d), bf16),
        ((nz, CORES, SLOT_DEV, 2, pad, d), bf16),
        ((nz, SLOT_DEV, 2, pad, d), bf16),
        ((2, nz // 2, SLOT_DEV, 2, pad, d), bf16),
        ((2, nz // 2, SLOT_DEV, 2, pad, d), bf16),
        ((nx, 2 * SLOT_DEV, tok_pad, d), bf16),
        ((nx, 2 * SLOT_DEV, tok_pad, d), bf16),
    ]
    copies = 2 * (nx - 1) + 6 * ny + 6 * nz
    query_grad, key_grad, value_grad = pl.pallas_call(
        functools.partial(kernel, nx, ny, nz),
        out_shape=(
            jax.ShapeDtypeStruct(queries.shape, bf16),
            jax.ShapeDtypeStruct(image_keys.shape, bf16),
            jax.ShapeDtypeStruct(image_values.shape, bf16),
        ),
        in_specs=[hbm, hbm, hbm, hbm, smem, smem, smem, smem],
        out_specs=(hbm, vmem, vmem),
        scratch_shapes=[pltpu.VMEM(shape, dtype) for shape, dtype in scratch] + [
            pltpu.SemaphoreType.DMA((copies,)),
            pltpu.SemaphoreType.DMA((copies,)),
            pltpu.SemaphoreType.DMA((4,)),
        ],
        compiler_params=pltpu.CompilerParams(
            collective_id=0, has_side_effects=True, vmem_limit_bytes=56 * 1024 * 1024
        ),
        name="cross_attention_backward",
    )(queries, out_grad, image_keys, image_values, text_len, tile_counts, tile_slots, gate_param)
    return (
        query_grad, jnp.transpose(key_grad, (1, 0, 2)), jnp.transpose(value_grad, (1, 0, 2))
    )


def solution(mesh):
    sizes = (mesh.shape["head"], mesh.shape["seq"], mesh.shape["img"] // CORES)
    return jax.shard_map(
        functools.partial(on_device, sizes),
        mesh=mesh,
        in_specs=(
            P("img", "seq", "head"),
            P("img", "seq", "head"),
            P("img"),
            P("img", ("seq", "head"), None),
            P("img", ("seq", "head"), None),
            P("img"),
            P("img", None),
            P(),
        ),
        out_specs=(
            P("img", "seq", "head"),
            P("img", ("seq", "head"), None),
            P("img", ("seq", "head"), None),
        ),
        check_vma=False,
    )
```

time: 160 us -> 131 us (0.82)
  Pallas kernels: 150 us -> 124 us
  local copies, waits for them, and re-layouts: 6.24 us -> 3.28 us
    pallas_call x1, Pallas kernels: 150 us -> 124 us  [on_device(): pl.pallas_call(functools.partial(kernel, nx, ny, nz), out_shape=(jax.Shap...]
    pallas_call x2 -> x0, local copies, waits for them, and re-layouts: 3.28 us -> none  [on_device(): pl.pallas_call(functools.partial(kernel, nx, ny, nz), out_shape=(jax.Shap...]
where the time goes in v2:
time: 131 us; the launch traced here: 130 us
  Pallas kernels  124 us (95%)
  local copies, waits for them, and re-layouts  3.28 us (3%)
  between operations  2.59 us (2%)
    pallas_call x1, Pallas kernels, on_device(): pl.pallas_call(functools.partial(kernel, nx, ny, nz), out_shape=(jax.Shap...  124 us
    unnamed x7, local copies, waits for them, and re-layouts  3.28 us

profile of v2, /device:TPU:1, one launch (start us, length us, event | category | flops | bytes accessed | tf_op | source)
XLA Modules:
  0.0 130.1 jit_solution(9677473400657364597)
XLA Ops:
  2.6 124.2 %cross_attention_backward.1 = (bf16[1,128,1024]{2,1,0:T(8,128)(2,1)}, bf16[50,2,512]{2,1,0:T(2,128)(2,1)}, bf16[50,2,512]{2,1,0:T(2,128)(2,1)}) custom-call(bf16[1,128,1024]{2,1,0:T(8,128)(2,1)} %q_hbm.1, bf16[1,128,1024]{2,1,0:T(8,128)(2,1)} %g_hbm.1, bf16[50,2,512]{2,1,0:T(2,128)(2,1)} %bitcast.6, bf16[50,2,512]{2,1,0:T(2,128)(2,1)} %bitcast.7, ...), custom_call_target="tpu_custom_call" | custom-call | tf_op jit(solution)/shard_map/cross_attention_backward/pallas_call | solution.py:441
  126.8 0.0 copy-start.1
  126.8 1.7 %copy.17 = bf16[1,128,1024]{2,1,0:T(8,128)(2,1)} copy(bf16[1,128,1024]{2,1,0:T(8,128)(2,1)} %get-tuple-element.12) | data formatting | bytes 524288
  128.5 0.0 copy-done.1
  128.5 0.0 copy-start
  128.5 0.6 copy.18
  129.1 0.3 copy-done
  129.4 0.6 copy.19
Async XLA Ops:
  126.8 1.7 %copy-start.1 = (bf16[50,2,512]{2,1,0:T(2,128)(2,1)S(1)}, bf16[50,2,512]{2,1,0:T(2,128)(2,1)}, u32[]{:S(2)}) copy-start(bf16[50,2,512]{2,1,0:T(2,128)(2,1)} %get-tuple-element.7) | copy-start | bytes 307204
  128.5 0.9 copy-start

commit v3 on v2

--- a/solution.py
+++ b/solution.py
@@ -14,8 +14,9 @@
 GROUP = 8
 CORES = 2
 SLOT_DEV = 2
-BLOCK = 256
+BLOCK = 512
 FAR = 1e30
+PIECES = 4
 
 
 def pad16(n):
@@ -27,7 +28,7 @@
     q_hbm, g_hbm, k_hbm, v_hbm, len_ref, count_ref, slot_ref, gate_ref,
     dq_hbm, dk_ref, dv_ref,
     q_ref, g_ref, k_ref, v_ref, dq_ref, head_out, head_in, tiles, keys, rowed,
-    stat_out, stat_in, final, terms, q_terms, q_own, y_out, y_in, own,
+    stat_out, stat_in, final, terms, q_terms, y_out, y_in, own,
     mine, twin, z_out, z_in, back_out, back_in,
     send_sem, recv_sem, local_sem,
 ):
@@ -66,7 +67,7 @@
     for device in partners:
         pl.semaphore_signal(barrier, inc=1, device_id=device, device_id_type=MESH)
 
-    started = []
+    started, returns = [], []
 
     def send(src, dst, device):
         index = len(started)
@@ -78,10 +79,9 @@
         started.append(copy)
         return copy
 
-    def run(steps, *rings):
+    def run(steps, ring):
         for _ in range(steps):
-            for ring in rings:
-                next(ring, None)
+            next(ring, None)
 
     for kv, ref in enumerate((k_ref, v_ref)):
         loads[kv].wait()
@@ -109,11 +109,11 @@
         half = n // 2
         copies = {}
         for t in range(1, half + 1):
-            for h in range(2):
+            for h in range(PIECES):
                 for way, step in enumerate((1, -1)):
                     if (way, h) in copies:
                         copies.pop((way, h)).wait_recv()
-                    if t < half or h == way:
+                    if t < half or h * 2 // PIECES == way:
                         source, target = ref(-step * (t - 1) % n, h), ref(-step * t % n, h)
                         copies[way, h] = send(source, target, at(step))
                 yield
@@ -130,15 +130,14 @@
                 tiles[0, 0, q // 2, q % 2, t * tok:(t + 1) * tok, :] = block
 
     def gather_z():
-        ring = gather(nz, at_z, lambda d, h: tiles.at[d, 0, h])
+        ring = gather(nz, at_z, lambda d, h: tiles.at[d, 0, h // 2, h % 2])
         twins = []
 
         def forward(d):
             twins.append(send(tiles.at[d, 0], tiles.at[d, 1], other_core))
 
         for t in range(1, nz // 2 + 1):
-            next(ring)
-            next(ring)
+            run(PIECES, ring)
             for d in [0] if t == 1 else [t - 1, -(t - 1) % nz]:
                 forward(d)
             yield
@@ -222,14 +221,14 @@
             score_grads = jnp.concatenate(score_grads, axis=0).astype(jnp.bfloat16)
             terms[0] += jnp.dot(score_grads, rowed[c, 0, b], preferred_element_type=jnp.float32)
             terms[1] += jnp.dot(weights, rowed[c, 1, b], preferred_element_type=jnp.float32)
-            q_terms[w, b] = lax.dot_general(
+            q_terms[c, b] = lax.dot_general(
                 score_grads, keys[0], (((0,), (0,)), ((), ())),
                 preferred_element_type=jnp.float32,
             )
 
         over(chunks, body)
 
-    def scatter(n, at, block, out, arrived, prepare, finish):
+    def scatter(n, pieces, at, block, out, arrived, prepare, finish):
         half = n // 2
         copies = {}
 
@@ -243,33 +242,28 @@
         for s in range(half):
             t = half - s
             prepare([half] if s == 0 else [t, n - t])
-            for h in range(2):
+            for h in range(pieces):
                 for way, step in enumerate((1, -1)):
-                    if s == 0 and h != way:
+                    if s == 0 and h * 2 // pieces != way:
                         continue
                     value = block(way if s > 0 else 0, step * t % n, h)
-                    out[way, s, h] = total(value, h, step * t).astype(out.dtype)
-                    copies[way, h] = send(out.at[way, s, h], arrived.at[way, s, h], at(step))
+                    place = (way, s, h)
+                    out[place] = total(value, h, step * t).astype(out.dtype)
+                    copies[way, h] = send(out.at[place], arrived.at[place], at(step))
             yield
         prepare([0])
-        for h in range(2):
+        for h in range(pieces):
             finish(h, total(block(0, 0, h), h, 0))
         yield
 
-    half_blocks = blocks // 2
-
     def query_block(w, d, h):
-        cut = slice(h * half_blocks, (h + 1) * half_blocks)
-        return q_own[cut] if d == 0 else q_terms[w, cut]
+        return q_terms[d, h]
 
     def query_finish(h, value):
-        value = value * grad_factor[None]
-        for i in range(half_blocks):
-            for r in range(0, BLOCK, rows):
-                g = ((h * half_blocks + i) * BLOCK + r) // rows
-                dq_ref[0, :, g * HEAD_DIM:(g + 1) * HEAD_DIM] = (
-                    value[i, r:r + rows].astype(jnp.bfloat16)
-                )
+        value = value * grad_factor
+        for r in range(0, BLOCK, rows):
+            g = (h * BLOCK + r) // rows
+            dq_ref[0, :, g * HEAD_DIM:(g + 1) * HEAD_DIM] = value[r:r + rows].astype(jnp.bfloat16)
 
     def build(d, side):
         for s in range(SLOT_DEV):
@@ -305,40 +299,44 @@
             for d in places:
                 from_twin[d].wait_recv()
 
-        def finish(s, value):
-            for kv in range(2):
-                for t in range(nx):
-                    back_out[t, 2 * s + kv, 0:tok, :] = value[kv, t * tok:(t + 1) * tok]
-
-        yield from scatter(
-            nz, at_z, lambda w, d, s: mine[d, 0, s] + twin[d, s], z_out, z_in, prepare, finish
-        )
+        def finish(h, value):
+            back_in[x, h, 0:tok, :] = value[0:tok]
+            for t in range(1, nx):
+                back_out[t, h, 0:tok, :] = value[t * tok:(t + 1) * tok]
+                returns.append(send(back_out.at[t, h], back_in.at[x, h], at_x(-t)))
+
+        def block(w, d, h):
+            return mine[d, 0, h // 2, h % 2] + twin[d, h // 2, h % 2]
+
+        yield from scatter(nz, PIECES, at_z, block, z_out, z_in, prepare, finish)
 
     z_half, y_half = nz // 2, ny // 2
-    y_ring = gather(ny, at_y, lambda d, h: rowed.at[d, h])
+    part_blocks = blocks // 2
+    y_ring = gather(
+        ny, at_y, lambda d, h: rowed.at[d, h // 2, pl.ds(h % 2 * part_blocks, part_blocks)]
+    )
     z_ring = gather_z()
-    run(2, y_ring)
+    run(PIECES, y_ring)
     collect()
     run(1, z_ring)
     terms[...] = jnp.zeros(terms.shape, jnp.float32)
-    y_steps = 2
     for step in range(z_half):
-        if y_steps < 2 * y_half - 2:
-            run(1, y_ring)
-            y_steps += 1
+        run(PIECES // 2, y_ring)
         run(1, z_ring)
+    passed = PIECES + z_half * PIECES // 2
+    if y_half > 2:
+        run(1, y_ring)
+        passed += 1
     run(1, z_ring)
-    swept = 0
-    while y_steps <= 2 * y_half:
-        arrived = (y_steps - 2) // 2 if y_steps <= 2 * y_half else y_half
-        first_sweep([0] if swept == 0 else [swept, ny - swept])
-        swept += 1
-        while y_steps <= 2 * y_half and (y_steps - 2) // 2 < swept:
-            run(1, y_ring)
-            y_steps += 1
-    while swept < y_half:
-        first_sweep([swept, ny - swept])
-        swept += 1
+    first_sweep([0])
+    for step in range(1, y_half):
+        missing = (step + 1) * PIECES - passed
+        ahead = 2 if step < y_half - 1 else PIECES
+        steps = max(missing, min(ahead, y_half * PIECES - passed))
+        run(steps, y_ring)
+        passed += steps
+        first_sweep([step, ny - step])
+    run(y_half * PIECES + 1 - passed, y_ring)
     first_sweep([y_half])
 
     stat_in[0] = stat_out[0]
@@ -358,26 +356,35 @@
     final[0, 1] = cross / total
     finals = {d: send(final.at[0], final.at[(ny - d) % ny], at_y(d)) for d in order}
 
-    def query_prepare(places):
-        for d in places:
+    def sweep_all(chunks):
+        for d in chunks:
             if d != 0:
                 finals[(ny - d) % ny].wait_recv()
-        if places != [0]:
-            second_sweep(places)
-
-    second_sweep([0])
-    q_own[...] = q_terms[0]
-    y_ring = scatter(ny, at_y, query_block, y_out, y_in, query_prepare, query_finish)
-    run(y_half, y_ring)
+        second_sweep(chunks)
+
     z_ring = scatter_z()
-    run(3, z_ring)
+    y_ring = scatter(
+        ny, blocks, at_y, query_block, y_out, y_in, lambda places: None, query_finish
+    )
+    sweep_all([0])
+    sweep_all([y_half])
     run(1, y_ring)
+    y_steps = 1
+    for t in range(y_half - 1, 0, -1):
+        sweep_all([t, ny - t])
+        if t == 2:
+            run(1, y_ring)
+            y_steps += 1
+    run(1, z_ring)
+    run(1, y_ring)
+    run(2, z_ring)
+    y_steps += 1
+    run(y_half - y_steps, y_ring)
+    run(max(z_half - 2, 0), z_ring)
+    run(2, y_ring)
     store = pltpu.make_async_copy(dq_ref, dq_hbm, local_sem.at[0])
     store.start()
     run(z_half, z_ring)
-
-    returns = [send(back_out.at[t], back_in.at[x], at_x(-t)) for t in range(1, nx)]
-    back_in[x] = back_out[0]
     for copy in returns:
         copy.wait_recv()
     for h in range(nx):
@@ -425,19 +432,18 @@
         ((ny, 3, blocks, 1, BLOCK), f32),
         ((ny, 2, blocks, 1, BLOCK), f32),
         ((2, span, d), f32),
-        ((2, blocks, BLOCK, d), f32),
-        ((blocks, BLOCK, d), f32),
-        ((2, ny // 2, 2, blocks // 2, BLOCK, d), bf16),
-        ((2, ny // 2, 2, blocks // 2, BLOCK, d), bf16),
+        ((ny, blocks, BLOCK, d), f32),
+        ((2, ny // 2, blocks, BLOCK, d), bf16),
+        ((2, ny // 2, blocks, BLOCK, d), bf16),
         ((MAX_TILES, 2, pad, d), bf16),
         ((nz, CORES, SLOT_DEV, 2, pad, d), bf16),
         ((nz, SLOT_DEV, 2, pad, d), bf16),
-        ((2, nz // 2, SLOT_DEV, 2, pad, d), bf16),
-        ((2, nz // 2, SLOT_DEV, 2, pad, d), bf16),
+        ((2, nz // 2, PIECES, pad, d), bf16),
+        ((2, nz // 2, PIECES, pad, d), bf16),
         ((nx, 2 * SLOT_DEV, tok_pad, d), bf16),
         ((nx, 2 * SLOT_DEV, tok_pad, d), bf16),
     ]
-    copies = 2 * (nx - 1) + 6 * ny + 6 * nz
+    copies = (PIECES + 1) * (nx - 1) + 2 * (PIECES + 1) * (ny + nz)
     query_grad, key_grad, value_grad = pl.pallas_call(
         functools.partial(kernel, nx, ny, nz),
         out_shape=(

time: 131 us -> 122 us (0.931)
  Pallas kernels: 124 us -> 114 us
    pallas_call x1, Pallas kernels: 124 us -> 114 us  [on_device(): pl.pallas_call(functools.partial(kernel, nx, ny, nz), out_shape=(jax.Shap...]
where the time goes in v3:
time: 122 us; the launch traced here: 120 us
  Pallas kernels  114 us (93%)
  local copies, waits for them, and re-layouts  3.28 us (3%)
  between operations  2.59 us (2%)
    pallas_call x1, Pallas kernels, on_device(): pl.pallas_call(functools.partial(kernel, nx, ny, nz), out_shape=(jax.Shap...  114 us
    unnamed x7, local copies, waits for them, and re-layouts  3.28 us

profile of v3, /device:TPU:1, one launch (start us, length us, event | category | flops | bytes accessed | tf_op | source)
XLA Modules:
  0.0 119.9 jit_solution(12032333601943001216)
XLA Ops:
  2.6 114.0 %cross_attention_backward.1 = (bf16[1,128,1024]{2,1,0:T(8,128)(2,1)}, bf16[50,2,512]{2,1,0:T(2,128)(2,1)}, bf16[50,2,512]{2,1,0:T(2,128)(2,1)}) custom-call(bf16[1,128,1024]{2,1,0:T(8,128)(2,1)} %q_hbm.1, bf16[1,128,1024]{2,1,0:T(8,128)(2,1)} %g_hbm.1, bf16[50,2,512]{2,1,0:T(2,128)(2,1)} %bitcast.6, bf16[50,2,512]{2,1,0:T(2,128)(2,1)} %bitcast.7, ...), custom_call_target="tpu_custom_call" | custom-call | tf_op jit(solution)/shard_map/cross_attention_backward/pallas_call | solution.py:447
  116.6 0.0 copy-start.1
  116.6 1.7 %copy.17 = bf16[1,128,1024]{2,1,0:T(8,128)(2,1)} copy(bf16[1,128,1024]{2,1,0:T(8,128)(2,1)} %get-tuple-element.12) | data formatting | bytes 524288
  118.3 0.0 copy-done.1
  118.3 0.0 copy-start
  118.3 0.6 copy.18
  118.9 0.3 copy-done
  119.2 0.6 copy.19
Async XLA Ops:
  116.6 1.7 %copy-start.1 = (bf16[50,2,512]{2,1,0:T(2,128)(2,1)S(1)}, bf16[50,2,512]{2,1,0:T(2,128)(2,1)}, u32[]{:S(2)}) copy-start(bf16[50,2,512]{2,1,0:T(2,128)(2,1)} %get-tuple-element.7) | copy-start | bytes 307204
  118.3 0.9 copy-start
